TPU v7x, 32 devices: a whole 2x2x4 slice. The times are simulated.
32 devices in a mesh: group: 2 (over x), expert: 16 (over z, y, core).
Axes of the slice: x: 2, y: 2, z: 4, core: 2. Of those that a mesh axis runs over, the one named last changes fastest.
Arguments:
- tokens: bfloat16 [2048, 1792], P(('group', 'expert')), parts along dimension 0, may hold values from -6 to 6
- shared_gate: bfloat16 [1792, 20480], P(None, 'expert'), may hold values from -0.125 to 0.125
- shared_up: bfloat16 [1792, 20480], P(None, 'expert'), may hold values from -0.125 to 0.125
- shared_down: bfloat16 [20480, 1792], P('expert'), may hold values from -0.0390625 to 0.0390625
- slab_gate: bfloat16 [16, 1792, 640], P('expert'), may hold values from -0.125 to 0.125
- slab_up: bfloat16 [16, 1792, 640], P('expert'), may hold values from -0.125 to 0.125
- slab_down: bfloat16 [16, 640, 1792], P('expert'), may hold values from -0.15625 to 0.15625
- picks: int32 [16, 16, 16], P('group', 'expert'), parts along dimension 0, may hold values from 0 to 63, as said below
- counts: int32 [16, 16], P('group', 'expert'), parts along dimension 0, may hold values from 1 to 16, 128 in all within a row
- gates: float32 [16, 16, 16], P('group', 'expert'), parts along dimension 0, may hold values from 0.1 to 1
Outputs:
- layer_out: bfloat16 [2048, 1792], P(('group', 'expert')), parts along dimension 0
There are 2 independent parts, one for each index of `group`. A program takes and returns all parts, laid end to end along the dimension named above; an argument that names none is the same for every part. Nothing has to cross between parts.
Inputs may be any that keep to these rules, and one draw needn't show every extreme that they name: `picks`: for each expert and source device the 16 entries are distinct rows; entries at or beyond that pair's count are ignored. For each expert the counts over the 16 source devices sum to 128.
All inputs are finite; a program needn't handle non-finite values.
Results may differ from a plain program's by a relative error of at most 0.0053.
Values may be sent and summed in bfloat16 or wider, within the bound.
A program may use at most 192 MiB of HBM per device.

v0:
```python
import jax
import jax.numpy as jnp
from jax import lax
from jax.sharding import PartitionSpec as P


def return_routed(contribution, sources, slot_count, features, onehot, experts, tok_dev):
    returned = lax.all_to_all(
        contribution.reshape(sources, slot_count, features),
        "expert",
        split_axis=0,
        concat_axis=0,
        tiled=True,
    )
    owner_table = (
        jnp.repeat(onehot, 2, axis=0)
        .reshape(2 * experts * slot_count, tok_dev)
        .astype(jnp.bfloat16)
    )
    return lax.dot_general(
        owner_table,
        returned.reshape(-1, features),
        (((0,), (0,)), ((), ())),
        preferred_element_type=jnp.float32,
    )


def on_device(
    tokens, shared_gate, shared_up, shared_down, slab_gate, slab_up, slab_down, picks, counts, gates
):
    tok_dev, features = tokens.shape
    own_picks = picks[:, 0, :]
    own_gates = gates[:, 0, :]
    experts, slot_count = own_picks.shape
    live_slot = lax.broadcasted_iota(jnp.int32, (experts, slot_count), 1) < counts
    local_rows = lax.broadcasted_iota(jnp.int32, (1, 1, tok_dev), 2)
    onehot = (own_picks[:, :, None] == local_rows) & live_slot[:, :, None]
    gate_total = jnp.sum(jnp.where(onehot, own_gates[:, :, None], 0.0), axis=(0, 1))
    divisor = jnp.maximum(gate_total, 1.0)
    weight = jnp.where(live_slot, own_gates / divisor[own_picks], 0.0).astype(jnp.bfloat16)
    sent_rows = jnp.where(live_slot[:, :, None], tokens[own_picks], jnp.zeros((), tokens.dtype))
    positions = own_picks.astype(jnp.float32).astype(jnp.bfloat16)
    weight_both = jnp.repeat(weight, 2, axis=0)
    position_both = jnp.repeat(positions, 2, axis=0)
    received, got_weight, got_position = (
        lax.all_to_all(
            jnp.repeat(sent_rows, 2, axis=0), "expert", split_axis=0, concat_axis=0, tiled=True
        ),
        lax.all_to_all(weight_both, "expert", split_axis=0, concat_axis=0, tiled=True),
        lax.all_to_all(position_both, "expert", split_axis=0, concat_axis=0, tiled=True),
    )
    sources = received.shape[0]
    flat_rows = received.reshape(sources * slot_count, features)
    gate_act = jnp.dot(flat_rows, slab_gate[0], preferred_element_type=jnp.float32)
    up_act = jnp.dot(flat_rows, slab_up[0], preferred_element_type=jnp.float32)
    slab_hidden = (jax.nn.silu(gate_act) * up_act).astype(jnp.bfloat16)
    slab_output = jnp.dot(slab_hidden, slab_down[0], preferred_element_type=jnp.float32)
    contribution = (slab_output * got_weight.reshape(-1, 1).astype(jnp.float32)).astype(
        jnp.bfloat16
    )
    piece = lax.all_gather(tokens, "expert", axis=0, tiled=True)
    gate_part = jnp.dot(piece, shared_gate, preferred_element_type=jnp.float32)
    up_part = jnp.dot(piece, shared_up, preferred_element_type=jnp.float32)
    shared_hidden = (jax.nn.silu(gate_part) * up_part).astype(jnp.bfloat16)
    layer_sum = lax.psum_scatter(
        jnp.dot(shared_hidden, shared_down, preferred_element_type=jnp.float32),
        "expert",
        scatter_dimension=0,
        tiled=True,
    )
    layer_sum = layer_sum + return_routed(
        contribution, sources, slot_count, features, onehot, experts, tok_dev
    )
    return layer_sum.astype(jnp.bfloat16)


def solution(mesh):
    in_specs = (
        P(("group", "expert"), None),
        P(None, "expert"),
        P(None, "expert"),
        P("expert", None),
        P("expert", None, None),
        P("expert", None, None),
        P("expert", None, None),
        P("group", "expert", None),
        P("group", "expert"),
        P("group", "expert", None),
    )
    out_specs = P(("group", "expert"), None)
    return jax.shard_map(
        on_device, mesh=mesh, in_specs=in_specs, out_specs=out_specs, check_vma=False
    )
```

profile of v0, /device:TPU:0, one launch (start us, length us, event | category | flops | bytes accessed | tf_op | source)
XLA Modules:
  0.0 202.9 jit_solution(13883174352881913723)
XLA Ops:
  6.5 0.7 all-gather.2.cloned.1.call-update
  7.3 52.6 %all-gather.2.cloned.1.call-done = bf16[1024,1792]{1,0:T(8,128)(2,1)} async-done(((bf16[64,1792]{1,0:T(8,128)(2,1)}), bf16[1024,1792]{1,0:T(8,128)(2,1)}) %all-gather.2.cloned.1.call-update) | async-done | bytes 3670032 | tf_op jit(solution)/shard_map/all_gather | solution.py:61
  59.9 10.6 %fusion.25 = f32[1024,1280]{1,0:T(8,128)} fusion(bf16[1024,1792]{1,0:T(8,128)(2,1)} %all-gather.2.cloned.1.call-done, bf16[1792,1280]{1,0:T(8,128)(2,1)} %param.11), kind=kOutput, calls=%fused_computation.33 | convolution fusion | flops 4697620480 | bytes 13500416 | tf_op jit(solution)/shard_map/dot_general | solution.py:62
  70.5 16.9 %fusion.13 = f32[1024,1792]{1,0:T(8,128)} fusion(bf16[1280,1792]{1,0:T(8,128)(2,1)} %param.13, f32[1024,1280]{1,0:T(8,128)} %fusion.25, bf16[1024,1792]{1,0:T(8,128)(2,1)} %all-gather.2.cloned.1.call-done, bf16[1792,1280]{1,0:T(8,128)(2,1)} %param.12), kind=kOutput, calls=%fused_computation.14 | convolution fusion | flops 9403105280 | bytes 25427968 | tf_op jit(solution)/shard_map/dot_general | solution.py:66
  87.4 0.6 copy-done.2
  88.0 0.1 reshape.84
  88.2 0.1 select_reduce_fusion
  88.4 1.2 gather_fusion.1
  89.7 0.6 copy.12
  90.4 3.7 %all-to-all-start.1 = ((bf16[16,1,16]{2,1,0:T(2,128)(2,1)}), bf16[16,1,16]{2,1,0:T(2,128)(2,1)S(1)}, u32[]{:S(2)}, u32[]{:S(2)}) async-start(bf16[16,1,16]{2,1,0:T(2,128)(2,1)} %copy.12), calls=%async_computation.2 | async-start | bytes 16384 | tf_op jit(solution)/shard_map/all_to_all | solution.py:49
  94.1 0.9 gather_fusion
  95.1 0.1 broadcast_select_fusion
  95.2 5.3 %all-to-all-done.1 = bf16[16,1,16]{2,1,0:T(2,128)(2,1)S(1)} async-done(((bf16[16,1,16]{2,1,0:T(2,128)(2,1)}), bf16[16,1,16]{2,1,0:T(2,128)(2,1)S(1)}, u32[]{:S(2)}, u32[]{:S(2)}) %all-to-all-start.1) | async-done | bytes 544 | tf_op jit(solution)/shard_map/all_to_all | solution.py:49
  100.4 1.0 broadcast_in_dim.44
  101.5 3.6 %all-to-all-start = ((bf16[16,16,1792]{2,1,0:T(8,128)(2,1)}), bf16[16,16,1792]{2,1,0:T(8,128)(2,1)S(1)}, u32[]{:S(2)}, u32[]{:S(2)}) async-start(bf16[16,16,1792]{2,1,0:T(8,128)(2,1)} %bitcast.5), calls=%async_computation.1 | async-start | bytes 1835008 | tf_op jit(solution)/shard_map/all_to_all | solution.py:46
  105.1 0.1 reshape.81
  105.2 24.8 %all-to-all-done = bf16[16,16,1792]{2,1,0:T(8,128)(2,1)S(1)} async-done(((bf16[16,16,1792]{2,1,0:T(8,128)(2,1)}), bf16[16,16,1792]{2,1,0:T(8,128)(2,1)S(1)}, u32[]{:S(2)}, u32[]{:S(2)}) %all-to-all-start) | async-done | bytes 917536 | tf_op jit(solution)/shard_map/all_to_all | solution.py:46
  130.0 3.4 %fusion.5 = f32[256,640]{1,0:T(8,128)} fusion(bf16[256,1792]{1,0:T(8,128)(2,1)S(1)} %bitcast.39, bf16[1,1792,640]{2,1,0:T(8,128)(2,1)} %param.14), kind=kOutput, calls=%fused_computation.10 | convolution fusion | flops 587202560 | bytes 3866624 | tf_op jit(solution)/shard_map/dot_general | solution.py:54
  133.5 4.4 %fusion = bf16[256,1792]{1,0:T(8,128)(2,1)} fusion(bf16[1,640,1792]{2,1,0:T(8,128)(2,1)S(1)} %copy-done, f32[256]{0:T(256)S(1)} %reshape.81, bf16[256,1792]{1,0:T(8,128)(2,1)S(1)} %bitcast.40, bf16[1,1792,640]{2,1,0:T(8,128)(2,1)} %param.15, f32[256,640]{1,0:T(8,128)} %fusion.5), kind=kOutput, calls=%fused_computation.4 | convolution fusion | flops 1176305664 | bytes 7078912 | tf_op jit(solution)/shard_map/dot_general | solution.py:57
  137.9 16.6 %all-to-all-start.2 = ((bf16[16,16,1792]{2,1,0:T(8,128)(2,1)}), bf16[16,16,1792]{2,1,0:T(8,128)(2,1)S(1)}, u32[]{:S(2)}, u32[]{:S(2)}) async-start(bf16[16,16,1792]{2,1,0:T(8,128)(2,1)} %bitcast.41), calls=%async_computation.3 | async-start | bytes 1835008 | tf_op jit(solution)/shard_map/all_to_all | solution.py:8
  154.6 0.1 fusion.22
  154.7 26.8 %all-to-all-done.2 = bf16[16,16,1792]{2,1,0:T(8,128)(2,1)S(1)} async-done(((bf16[16,16,1792]{2,1,0:T(8,128)(2,1)}), bf16[16,16,1792]{2,1,0:T(8,128)(2,1)S(1)}, u32[]{:S(2)}, u32[]{:S(2)}) %all-to-all-start.2) | async-done | bytes 917536 | tf_op jit(solution)/shard_map/all_to_all | solution.py:8
  181.5 12.5 %reduce-scatter.2.cloned.1.call-done = f32[64,1792]{1,0:T(8,128)} async-done(((f32[1024,1792]{1,0:T(8,128)}), f32[64,1792]{1,0:T(8,128)}) %reduce-scatter.2.cloned.1.call-update) | async-done | bytes 458768 | tf_op jit(solution)/shard_map/reduce_scatter | solution.py:65
  194.0 2.0 %fusion.1 = bf16[64,1792]{1,0:T(8,128)(2,1)} fusion(f32[64,1792]{1,0:T(8,128)} %reduce-scatter.2.cloned.1.call-done, pred[256,64]{1,0:T(8,128)(4,1)S(1)} %bitcast.42, bf16[256,1792]{1,0:T(8,128)(2,1)S(1)} %bitcast.37), kind=kOutput, calls=%fused_computation.6 | convolution fusion | flops 58949632 | bytes 1622016 | tf_op jit(solution)/shard_map/dot_general | solution.py:20
  (21 shorter events, 0.4 us)
Async XLA Ops:
  6.5 126.9 %copy-start = (bf16[1,640,1792]{2,1,0:T(8,128)(2,1)S(1)}, bf16[1,640,1792]{2,1,0:T(8,128)(2,1)}, u32[]{:S(2)}) copy-start(bf16[1,640,1792]{2,1,0:T(8,128)(2,1)} %param.16) | copy-start | bytes 6881284
  6.5 53.3 %all-gather.2.cloned.1.call-start = ((), (), s32[]{:S(2)}) async-start(), calls=%async_computation.4 | async-start | bytes 3899392 | tf_op jit(solution)/shard_map/all_gather | solution.py:61
  7.3 186.8 %reduce-scatter.2.cloned.1.call-start = ((), (), s32[]{:S(2)}) async-start(), calls=%async_computation.5 | async-start | bytes 7798784 | tf_op jit(solution)/shard_map/reduce_scatter | solution.py:65
  87.3 0.7 copy-start.2
  87.3 0.8 copy-start.4
  87.3 0.9 copy-start.3
  87.4 6.8 %copy-start.1 = (bf16[64,1792]{1,0:T(8,128)(2,1)S(1)}, bf16[64,1792]{1,0:T(8,128)(2,1)}, u32[]{:S(2)}) copy-start(bf16[64,1792]{1,0:T(8,128)(2,1)} %param.10) | copy-start | bytes 688132
  90.4 10.1 %all-to-all-start.1 = ((bf16[16,1,16]{2,1,0:T(2,128)(2,1)}), bf16[16,1,16]{2,1,0:T(2,128)(2,1)S(1)}, u32[]{:S(2)}, u32[]{:S(2)}) async-start(bf16[16,1,16]{2,1,0:T(2,128)(2,1)} %copy.12), calls=%async_computation.2 | async-start | bytes 16384 | tf_op jit(solution)/shard_map/all_to_all | solution.py:49
  101.5 28.6 %all-to-all-start = ((bf16[16,16,1792]{2,1,0:T(8,128)(2,1)}), bf16[16,16,1792]{2,1,0:T(8,128)(2,1)S(1)}, u32[]{:S(2)}, u32[]{:S(2)}) async-start(bf16[16,16,1792]{2,1,0:T(8,128)(2,1)} %bitcast.5), calls=%async_computation.1 | async-start | bytes 1835008 | tf_op jit(solution)/shard_map/all_to_all | solution.py:46
  137.9 43.6 %all-to-all-start.2 = ((bf16[16,16,1792]{2,1,0:T(8,128)(2,1)}), bf16[16,16,1792]{2,1,0:T(8,128)(2,1)S(1)}, u32[]{:S(2)}, u32[]{:S(2)}) async-start(bf16[16,16,1792]{2,1,0:T(8,128)(2,1)} %bitcast.41), calls=%async_computation.3 | async-start | bytes 1835008 | tf_op jit(solution)/shard_map/all_to_all | solution.py:8
Sparse Core Ops, SparseCore 0:
  9.6 50.1 all-gather.1
  87.5 106.4 reduce-scatter.1
where the time goes:
time: 203 us
  waiting for transfers between devices  123 us (61%)
  matrix products  37.4 us (18%)
  starting transfers between devices  24 us (12%)
  between operations  13.5 us (7%)
  local copies, waits for them, and re-layouts  4.7 us (2%)
    all_gather x1, waiting for transfers between devices, on_device(): piece = lax.all_gather(tokens, 'expert', axis=0, tiled=True)  52.6 us
    all_to_all x1, waiting for transfers between devices, return_routed(): lax.all_to_all(contribution.reshape(sources, slot_count, features), 'expe...  26.8 us
    all_to_all x1, waiting for transfers between devices, on_device(): lax.all_to_all(jnp.repeat(sent_rows, 2, axis=0), 'expert', split_axis=0,...  24.8 us
    dot_general x1, matrix products, on_device(): jnp.dot(shared_hidden, shared_down, preferred_element_type=jnp.float32)  16.9 us
    all_to_all x1, starting transfers between devices, return_routed(): lax.all_to_all(contribution.reshape(sources, slot_count, features), 'expe...  16.6 us
    reduce_scatter x1, waiting for transfers between devices, on_device(): lax.psum_scatter(jnp.dot(shared_hidden, shared_down, preferred_element_ty...  12.5 us
    dot_general x1, matrix products, on_device(): gate_part = jnp.dot(piece, shared_gate, preferred_element_type=jnp.float32)  10.6 us
    all_to_all x1, waiting for transfers between devices, on_device(): lax.all_to_all(weight_both, 'expert', split_axis=0, concat_axis=0, tiled=...  5.28 us
  transfers between devices with their start and end apart: 5, of which 5 were waited for; matrix products, arithmetic and copies ran while one was open for 6% of the time, Pallas kernels for 0%

commit v1 on v0

--- a/solution.py
+++ b/solution.py
@@ -1,7 +1,344 @@
 import jax
 import jax.numpy as jnp
 from jax import lax
+from jax.experimental import pallas as pl
+from jax.experimental.pallas import tpu as pltpu
 from jax.sharding import PartitionSpec as P
+
+LINE = 4
+LANES = 128
+F32 = jnp.float32
+BF16 = jnp.bfloat16
+
+
+def dot(a, b):
+    return jnp.dot(a, b, preferred_element_type=F32)
+
+
+def silu_mul(g, u):
+    return g / (1.0 + jnp.exp(-g)) * u
+
+
+def routing_columns(picks_ref, counts_ref, gates_ref, rows):
+    experts, _, slots = picks_ref.shape
+    row = lax.broadcasted_iota(jnp.int32, (rows, slots), 0)
+    slot = lax.broadcasted_iota(jnp.int32, (rows, slots), 1)
+    lane = lax.broadcasted_iota(jnp.int32, (rows, LANES), 1)
+    total = jnp.zeros((rows, 1), F32)
+    columns = []
+    for e in range(experts):
+        hit = (picks_ref[e] == row) & (slot < counts_ref[e : e + 1, :])
+        gate = jnp.sum(jnp.where(hit, gates_ref[e], 0.0), axis=1, keepdims=True)
+        code = jnp.sum(jnp.where(hit, (slot + 1).astype(F32), 0.0), axis=1, keepdims=True)
+        total = total + gate
+        columns.append((gate, code))
+    divisor = jnp.maximum(total, 1.0)
+    meta = jnp.zeros((rows, LANES), F32)
+    for e, (gate, code) in enumerate(columns):
+        meta = jnp.where(lane == e, gate / divisor, meta)
+        meta = jnp.where(lane == experts + e, code, meta)
+    return meta.astype(BF16)
+
+
+def kernel(
+    tokens, shared_gate, shared_up, shared_down, slab_gate, slab_up, slab_down, picks, counts, gates,
+    out,
+    w_gate, w_up, w_down, r_gate, r_up, r_down,
+    tok, hidden, routed_x, routed_hidden, routed_out, scatter,
+    part, core_in, y_out, y_in, y_keep, z_out, z_in,
+    load_sem, tok_recv, up_send, down_send, y_send, c_send, c_send_y,
+    rc_send, rc_recv, ry_send, ry_recv, rz_send, rz_recv,
+):
+    me = lax.axis_index("expert")
+    z, y, c = me // 4, (me // 2) % 2, me % 2
+    half = z // 2
+    near = z + half * (3 - 2 * z)
+    experts, _, slots = picks.shape
+    rows, width = tokens.shape
+    expert = me // 2
+    y_peer, c_peer = me + 2 - 4 * y, me + 1 - 2 * c
+
+    def mirror(o):
+        return o + half * (3 - 2 * o)
+
+    arrive = [mirror(near), mirror(1 - near), mirror(2), mirror(3)]
+    leave = [mirror(3), mirror(2 - 2 * near), mirror(1 + near), mirror(near)]
+
+    own = pltpu.make_async_copy(tokens, tok.at[me, :, :width], load_sem.at[6])
+    own.start()
+    loads = [
+        pltpu.make_async_copy(src, dst, load_sem.at[i])
+        for i, (src, dst) in enumerate(
+            [
+                (shared_gate, w_gate),
+                (shared_up, w_up),
+                (slab_gate.at[0], r_gate),
+                (slab_up.at[0], r_up),
+                (slab_down.at[0], r_down),
+                (shared_down, w_down),
+            ]
+        )
+    ]
+    barrier = pltpu.get_barrier_semaphore()
+
+    def greet(target):
+        pl.semaphore_signal(barrier, inc=1, device_id={"expert": target})
+
+    greet(y_peer)
+    greet(c_peer)
+
+    @pl.when(z < LINE - 1)
+    def _():
+        greet(me + 4)
+
+    @pl.when(z > 0)
+    def _():
+        greet(me - 4)
+
+    for load in loads:
+        load.start()
+    meta = routing_columns(picks, counts, gates, rows)
+    own.wait()
+    tok[me, :, width:] = meta
+    pl.semaphore_wait(barrier, 3 + near)
+
+    def block_copy(s, target, send_sem):
+        return pltpu.make_async_remote_copy(
+            src_ref=tok.at[s], dst_ref=tok.at[s], send_sem=send_sem, recv_sem=tok_recv.at[s],
+            device_id={"expert": target},
+        )
+
+    def column_copies(zt, act, along=True):
+        s = zt * 4 + y * 2 + c
+
+        if along:
+
+            @pl.when((zt <= z) & (z < LINE - 1))
+            def _():
+                act(block_copy(s, me + 4, up_send.at[zt]))
+
+            @pl.when((zt >= z) & (z > 0))
+            def _():
+                act(block_copy(s, me - 4, down_send.at[zt]))
+
+        act(block_copy(s, y_peer, y_send.at[zt]))
+        act(block_copy(s, c_peer, c_send.at[zt]))
+
+    def start(copy):
+        copy.start()
+
+    def wait_send(copy):
+        copy.wait_send()
+
+    def got(s):
+        block_copy(s, c_peer, c_send.at[0]).wait_recv()
+
+    def line_step(zt):
+        got(zt * 4 + y * 2 + c)
+        column_copies(zt, start)
+
+    def layer_ready(zt):
+        s = zt * 4 + (1 - y) * 2 + c
+        got(s)
+        block_copy(s, c_peer, c_send_y.at[zt]).start()
+        got(zt * 4 + 1 - c)
+        got(zt * 4 + 3 - c)
+
+    def first_half(zt):
+        def tile(n, _):
+            columns = pl.ds(pl.multiple_of(n * 256, 256), 256)
+            x = tok[pl.ds(zt * 4, 4), :, :width].reshape(4 * rows, width)
+            g = dot(x, w_gate[:, columns])
+            u = dot(x, w_up[:, columns])
+            hidden[zt, :, columns] = silu_mul(g, u).astype(BF16)
+            return 0
+
+        lax.fori_loop(0, w_gate.shape[1] // 256, tile, 0)
+        info = tok[pl.ds(zt * 4, 4), :, width:].reshape(4 * rows, LANES)
+        slots4 = 4 * slots
+        lane_r = lax.broadcasted_iota(jnp.int32, (slots4, LANES), 1)
+        pick_code = jnp.where(lane_r == experts + expert, 1.0, 0.0).astype(BF16)
+        pick_weight = jnp.where(lane_r == expert, 1.0, 0.0).astype(BF16)
+        nt = (((1,), (1,)), ((), ()))
+        code_t = lax.dot_general(pick_code, info, nt, preferred_element_type=F32)
+        code = lax.dot_general(info, pick_code, nt, preferred_element_type=F32)
+        weight = lax.dot_general(info, pick_weight, nt, preferred_element_type=F32)
+
+        def match(codes, slot_dim):
+            slot = lax.broadcasted_iota(jnp.int32, codes.shape, slot_dim)
+            token = lax.broadcasted_iota(jnp.int32, codes.shape, 1 - slot_dim)
+            return (codes == (slot % slots + 1).astype(F32)) & (slot // slots == token // rows)
+
+        scatter[zt] = jnp.where(match(code, 1), weight, 0.0).astype(BF16)
+        gather = jnp.where(match(code_t, 0), 1.0, 0.0).astype(BF16)
+        x = tok[pl.ds(zt * 4, 4), :, :width].reshape(4 * rows, width)
+        routed_x[zt] = dot(gather, x).astype(BF16)
+
+    column_copies(arrive[0], start)
+    line_step(arrive[1])
+
+    @pl.when(near == 1)
+    def _():
+        line_step(arrive[2])
+
+    layer_ready(arrive[0])
+    loads[0].wait()
+    loads[1].wait()
+    first_half(arrive[0])
+
+    @pl.when(near == 0)
+    def _():
+        line_step(arrive[2])
+
+    layer_ready(arrive[1])
+    first_half(arrive[1])
+    line_step(arrive[3])
+    layer_ready(arrive[2])
+    first_half(arrive[2])
+    layer_ready(arrive[3])
+    first_half(arrive[3])
+
+    for load in loads[2:]:
+        load.wait()
+    picked = LINE * 4 * slots
+    hs = r_gate.shape[1]
+    for low in range(0, hs, 256):
+        high = min(hs, low + 256)
+        x = routed_x[...].reshape(picked, width)
+        g = dot(x, r_gate[:, low:high])
+        u = dot(x, r_up[:, low:high])
+        routed_hidden[:, low:high] = silu_mul(g, u).astype(BF16)
+
+    def routed_tile(n, _):
+        columns = pl.ds(pl.multiple_of(n * 256, 256), 256)
+        o = dot(routed_hidden[...], r_down[:, columns])
+        routed_out[:, :, columns] = o.reshape(LINE, 4 * slots, 256).astype(BF16)
+        return 0
+
+    lax.fori_loop(0, width // 256, routed_tile, 0)
+
+    def second_half(zt):
+        def tile(n, _):
+            columns = pl.ds(pl.multiple_of(n * 256, 256), 256)
+            p = dot(hidden[zt], w_down[:, columns]) + dot(scatter[zt], routed_out[zt, :, columns])
+            p = p.astype(BF16)
+            for b in range(4):
+                part[zt, b % 2, b // 2, :, columns] = p[b * rows : (b + 1) * rows]
+            return 0
+
+        lax.fori_loop(0, width // 256, tile, 0)
+
+    def core_copy(zt):
+        return pltpu.make_async_remote_copy(
+            src_ref=part.at[zt, 1 - c], dst_ref=core_in.at[zt], send_sem=rc_send.at[zt],
+            recv_sem=rc_recv.at[zt], device_id={"expert": c_peer},
+        )
+
+    def y_copy(zt):
+        return pltpu.make_async_remote_copy(
+            src_ref=y_out.at[zt], dst_ref=y_in.at[zt], send_sem=ry_send.at[zt],
+            recv_sem=ry_recv.at[zt], device_id={"expert": y_peer},
+        )
+
+    def z_copy(zt, way, target):
+        return pltpu.make_async_remote_copy(
+            src_ref=z_out.at[zt], dst_ref=z_in.at[way, zt], send_sem=rz_send.at[zt],
+            recv_sem=rz_recv.at[way, zt], device_id={"expert": target},
+        )
+
+    def y_stage(zt):
+        core_copy(zt).wait_recv()
+        y_out[zt] = (part[zt, c, 1 - y].astype(F32) + core_in[zt, 1 - y].astype(F32)).astype(BF16)
+        y_copy(zt).start()
+        y_keep[zt] = part[zt, c, y].astype(F32) + core_in[zt, y].astype(F32)
+
+    def z_stage(zt, last):
+        y_copy(zt).wait_recv()
+        y_keep[zt] += y_in[zt].astype(F32)
+
+        @pl.when((zt >= z) & (z > 0))
+        def _():
+            z_copy(zt, 0, me - 4).wait_recv()
+            y_keep[zt] += z_in[0, zt].astype(F32)
+
+        @pl.when((zt <= z) & (z < LINE - 1))
+        def _():
+            z_copy(zt, 1, me + 4).wait_recv()
+            y_keep[zt] += z_in[1, zt].astype(F32)
+
+        if last:
+            out[...] = y_keep[zt].astype(BF16)
+        else:
+            z_out[zt] = y_keep[zt].astype(BF16)
+
+            @pl.when(zt > z)
+            def _():
+                z_copy(zt, 0, me + 4).start()
+
+            @pl.when(zt < z)
+            def _():
+                z_copy(zt, 1, me - 4).start()
+
+    for i in range(LINE):
+        second_half(leave[i])
+        core_copy(leave[i]).start()
+        if i > 0:
+            y_stage(leave[i - 1])
+    y_stage(leave[-1])
+    for i in range(LINE):
+        z_stage(leave[i], i == LINE - 1)
+
+    for i in range(LINE):
+        column_copies(arrive[i], wait_send)
+        block_copy(arrive[i] * 4 + (1 - y) * 2 + c, c_peer, c_send_y.at[arrive[i]]).wait_send()
+        core_copy(leave[i]).wait_send()
+        y_copy(leave[i]).wait_send()
+        if i < LINE - 1:
+            z_copy(leave[i], 0, y_peer).wait_send()
+
+
+def fused(
+    tokens, shared_gate, shared_up, shared_down, slab_gate, slab_up, slab_down, picks, counts, gates
+):
+    rows, width = tokens.shape
+    hid = shared_gate.shape[1]
+    hs = slab_gate.shape[2]
+    slots = picks.shape[2]
+    any_spec = pl.BlockSpec(memory_space=pl.ANY)
+    vmem_spec = pl.BlockSpec(memory_space=pltpu.VMEM)
+    dma = pltpu.SemaphoreType.DMA
+    vm = pltpu.VMEM
+    flops = 2 * 16 * rows * width * hid * 3
+    return pl.pallas_call(
+        kernel,
+        out_shape=jax.ShapeDtypeStruct((rows, width), BF16),
+        in_specs=[any_spec] * 7 + [vmem_spec] * 3,
+        out_specs=vmem_spec,
+        scratch_shapes=[
+            vm((width, hid), BF16), vm((width, hid), BF16), vm((hid, width), BF16),
+            vm((width, hs), BF16), vm((width, hs), BF16), vm((hs, width), BF16),
+            vm((4 * LINE, rows, width + LANES), BF16),
+            vm((LINE, 4 * rows, hid), BF16),
+            vm((LINE, 4 * slots, width), BF16),
+            vm((LINE * 4 * slots, hs), BF16),
+            vm((LINE, 4 * slots, width), BF16),
+            vm((LINE, 4 * rows, 4 * slots), BF16),
+            vm((LINE, 2, 2, rows, width), BF16),
+            vm((LINE, 2, rows, width), BF16),
+            vm((LINE, rows, width), BF16),
+            vm((LINE, rows, width), BF16),
+            vm((LINE, rows, width), F32),
+            vm((LINE, rows, width), BF16),
+            vm((2, LINE, rows, width), BF16),
+            dma((7,)), dma((4 * LINE,)), dma((LINE,)), dma((LINE,)), dma((LINE,)), dma((LINE,)),
+            dma((LINE,)),
+            dma((LINE,)), dma((LINE,)), dma((LINE,)), dma((LINE,)), dma((LINE,)), dma((2, LINE)),
+        ],
+        compiler_params=pltpu.CompilerParams(
+            collective_id=0, has_side_effects=True, vmem_limit_bytes=60 * 1024 * 1024
+        ),
+        cost_estimate=pl.CostEstimate(flops=flops, bytes_accessed=21000000, transcendentals=0),
+    )(tokens, shared_gate, shared_up, shared_down, slab_gate, slab_up, slab_down, picks, counts, gates)
 
 
 def return_routed(contribution, sources, slot_count, features, onehot, experts, tok_dev):
@@ -88,6 +425,7 @@
         P("group", "expert", None),
     )
     out_specs = P(("group", "expert"), None)
+    body = fused if mesh.shape["expert"] == 4 * LINE else on_device
     return jax.shard_map(
-        on_device, mesh=mesh, in_specs=in_specs, out_specs=out_specs, check_vma=False
-    )
+        body, mesh=mesh, in_specs=in_specs, out_specs=out_specs, check_vma=False
+    )

time: 203 us -> 81.8 us (0.40)
  waiting for transfers between devices: 123 us -> 0 us
  Pallas kernels: 0 us -> 78.6 us
  matrix products: 37.4 us -> 0 us
  starting transfers between devices: 24 us -> 0 us
  between operations: 13.5 us -> 0.01 us
    pallas_call x0 -> x1, Pallas kernels: none -> 78.6 us  [fused(): pl.pallas_call(kernel, out_shape=jax.ShapeDtypeStruct((rows, width), BF16...]
    all_to_all x3 -> x0, waiting for transfers between devices: 56.9 us -> none  [the longest x1 26.8 us: return_routed(): lax.all_to_all(contribution.reshape(sources, slot_count, features), 'expe...]
    all_gather x1 -> x0, waiting for transfers between devices: 52.6 us -> none  [on_device(): piece = lax.all_gather(tokens, 'expert', axis=0, tiled=True)]
    dot_general x5 -> x0, matrix products: 37.4 us -> none  [the longest x1 16.9 us: on_device(): jnp.dot(shared_hidden, shared_down, preferred_element_type=jnp.float32)]
    all_to_all x3 -> x0, starting transfers between devices: 24 us -> none  [the longest x1 16.6 us: return_routed(): lax.all_to_all(contribution.reshape(sources, slot_count, features), 'expe...]
    reduce_scatter x1 -> x0, waiting for transfers between devices: 12.5 us -> none  [on_device(): lax.psum_scatter(jnp.dot(shared_hidden, shared_down, preferred_element_ty...]
    unnamed x10 -> x2, local copies, waits for them, and re-layouts: 0.66 us -> 2.96 us
    gather x3 -> x0, local copies, waits for them, and re-layouts: 2.24 us -> none  [the longest x2 1.3 us: on_device(): divisor[own_picks]]
  transfers between devices with their start and end apart: 5 -> 0, of which waited for: 5 -> 0; matrix products, arithmetic and copies ran while one was open for 6% -> 0% of each run, Pallas kernels for 0% -> 0%
where the time goes in v1:
time: 81.8 us; the launch traced here: 81.6 us
  Pallas kernels  78.6 us (96%)
  local copies, waits for them, and re-layouts  2.96 us (4%)
    pallas_call x1, Pallas kernels, fused(): pl.pallas_call(kernel, out_shape=jax.ShapeDtypeStruct((rows, width), BF16...  78.6 us
    unnamed x2, local copies, waits for them, and re-layouts  2.96 us

profile of v1, /device:TPU:0, one launch (start us, length us, event | category | flops | bytes accessed | tf_op | source)
XLA Modules:
  0.0 81.6 jit_solution(8583970077623258130)
XLA Ops:
  0.0 1.3 %copy.11.counts = s32[8,1]{1,0:T(8,128)} copy(s32[8,1]{0,1:T(1,128)} %param.18) | data formatting | bytes 64 | tf_op args[8]
  1.3 78.6 %shard_map.100 = bf16[64,1792]{1,0:T(8,128)(2,1)} custom-call(bf16[64,1792]{1,0:T(8,128)(2,1)} %tokens.1, bf16[1792,1280]{1,0:T(8,128)(2,1)} %shared_gate.1, bf16[1792,1280]{1,0:T(8,128)(2,1)} %shared_up.1, bf16[1280,1792]{1,0:T(8,128)(2,1)} %shared_down.1, bf16[1,1792,640]{2,1,0:T(8,128)(2,1)} %slab_gate.1, bf16[1,1792,640]{2,1,0:T(8,128)(2,1)} %slab_up.1, ...), custom_call_target="tpu_custom_call" | custom-call | flops 14092861440 | bytes 21000000 | tf_op jit(solution)/shard_map/pallas_call | solution.py:312
  80.0 1.6 %copy.13 = bf16[64,1792]{1,0:T(8,128)(2,1)} copy(bf16[64,1792]{1,0:T(8,128)(2,1)} %shard_map.100) | data formatting | bytes 458752

commit v2 on v1

--- a/solution.py
+++ b/solution.py
@@ -54,7 +54,7 @@
     half = z // 2
     near = z + half * (3 - 2 * z)
     experts, _, slots = picks.shape
-    rows, width = tokens.shape
+    rows, width = 2 * tokens.shape[1], tokens.shape[2]
     expert = me // 2
     y_peer, c_peer = me + 2 - 4 * y, me + 1 - 2 * c
 
@@ -62,9 +62,9 @@
         return o + half * (3 - 2 * o)
 
     arrive = [mirror(near), mirror(1 - near), mirror(2), mirror(3)]
-    leave = [mirror(3), mirror(2 - 2 * near), mirror(1 + near), mirror(near)]
-
-    own = pltpu.make_async_copy(tokens, tok.at[me, :, :width], load_sem.at[6])
+    leave = [arrive[2], arrive[3], arrive[1], arrive[0]]
+
+    own = pltpu.make_async_copy(tokens, tok.at[me, :, :, :width], load_sem.at[6])
     own.start()
     loads = [
         pltpu.make_async_copy(src, dst, load_sem.at[i])
@@ -95,34 +95,30 @@
     def _():
         greet(me - 4)
 
-    for load in loads:
-        load.start()
     meta = routing_columns(picks, counts, gates, rows)
     own.wait()
-    tok[me, :, width:] = meta
+    tok[me, :, :, width:] = meta.reshape(2, rows // 2, LANES)
     pl.semaphore_wait(barrier, 3 + near)
 
-    def block_copy(s, target, send_sem):
+    def block_copy(s, h, target, send_sem):
         return pltpu.make_async_remote_copy(
-            src_ref=tok.at[s], dst_ref=tok.at[s], send_sem=send_sem, recv_sem=tok_recv.at[s],
+            src_ref=tok.at[s, h], dst_ref=tok.at[s, h], send_sem=send_sem, recv_sem=tok_recv.at[s, h],
             device_id={"expert": target},
         )
 
-    def column_copies(zt, act, along=True):
+    def column_copies(zt, h, act):
         s = zt * 4 + y * 2 + c
 
-        if along:
-
-            @pl.when((zt <= z) & (z < LINE - 1))
-            def _():
-                act(block_copy(s, me + 4, up_send.at[zt]))
-
-            @pl.when((zt >= z) & (z > 0))
-            def _():
-                act(block_copy(s, me - 4, down_send.at[zt]))
-
-        act(block_copy(s, y_peer, y_send.at[zt]))
-        act(block_copy(s, c_peer, c_send.at[zt]))
+        @pl.when((zt <= z) & (z < LINE - 1))
+        def _():
+            act(block_copy(s, h, me + 4, up_send.at[zt, h]))
+
+        @pl.when((zt >= z) & (z > 0))
+        def _():
+            act(block_copy(s, h, me - 4, down_send.at[zt, h]))
+
+        act(block_copy(s, h, y_peer, y_send.at[zt, h]))
+        act(block_copy(s, h, c_peer, c_send.at[zt, h]))
 
     def start(copy):
         copy.start()
@@ -130,31 +126,36 @@
     def wait_send(copy):
         copy.wait_send()
 
-    def got(s):
-        block_copy(s, c_peer, c_send.at[0]).wait_recv()
-
-    def line_step(zt):
-        got(zt * 4 + y * 2 + c)
-        column_copies(zt, start)
-
-    def layer_ready(zt):
+    def got(s, h):
+        block_copy(s, h, c_peer, c_send.at[0, 0]).wait_recv()
+
+    def line_step(zt, h):
+        got(zt * 4 + y * 2 + c, h)
+        column_copies(zt, h, start)
+
+    def y_step(zt, h):
         s = zt * 4 + (1 - y) * 2 + c
-        got(s)
-        block_copy(s, c_peer, c_send_y.at[zt]).start()
-        got(zt * 4 + 1 - c)
-        got(zt * 4 + 3 - c)
-
-    def first_half(zt):
+        got(s, h)
+        block_copy(s, h, c_peer, c_send_y.at[zt, h]).start()
+
+    def core_step(zt):
+        for h in range(2):
+            got(zt * 4 + 1 - c, h)
+            got(zt * 4 + 3 - c, h)
+
+    def first_half(i):
+        zt = arrive[i]
+
         def tile(n, _):
             columns = pl.ds(pl.multiple_of(n * 256, 256), 256)
-            x = tok[pl.ds(zt * 4, 4), :, :width].reshape(4 * rows, width)
+            x = tok[pl.ds(zt * 4, 4), :, :, :width].reshape(4 * rows, width)
             g = dot(x, w_gate[:, columns])
             u = dot(x, w_up[:, columns])
             hidden[zt, :, columns] = silu_mul(g, u).astype(BF16)
             return 0
 
         lax.fori_loop(0, w_gate.shape[1] // 256, tile, 0)
-        info = tok[pl.ds(zt * 4, 4), :, width:].reshape(4 * rows, LANES)
+        info = tok[pl.ds(zt * 4, 4), :, :, width:].reshape(4 * rows, LANES)
         slots4 = 4 * slots
         lane_r = lax.broadcasted_iota(jnp.int32, (slots4, LANES), 1)
         pick_code = jnp.where(lane_r == experts + expert, 1.0, 0.0).astype(BF16)
@@ -171,130 +172,188 @@
 
         scatter[zt] = jnp.where(match(code, 1), weight, 0.0).astype(BF16)
         gather = jnp.where(match(code_t, 0), 1.0, 0.0).astype(BF16)
-        x = tok[pl.ds(zt * 4, 4), :, :width].reshape(4 * rows, width)
-        routed_x[zt] = dot(gather, x).astype(BF16)
-
-    column_copies(arrive[0], start)
-    line_step(arrive[1])
-
-    @pl.when(near == 1)
-    def _():
-        line_step(arrive[2])
-
-    layer_ready(arrive[0])
-    loads[0].wait()
-    loads[1].wait()
-    first_half(arrive[0])
-
-    @pl.when(near == 0)
-    def _():
-        line_step(arrive[2])
-
-    layer_ready(arrive[1])
-    first_half(arrive[1])
-    line_step(arrive[3])
-    layer_ready(arrive[2])
-    first_half(arrive[2])
-    layer_ready(arrive[3])
-    first_half(arrive[3])
-
-    for load in loads[2:]:
-        load.wait()
-    picked = LINE * 4 * slots
+        x = tok[pl.ds(zt * 4, 4), :, :, :width].reshape(4 * rows, width)
+        routed_x[i * 4 * slots : (i + 1) * 4 * slots] = dot(gather, x).astype(BF16)
+
+    picked = 4 * slots
     hs = r_gate.shape[1]
-    for low in range(0, hs, 256):
-        high = min(hs, low + 256)
-        x = routed_x[...].reshape(picked, width)
-        g = dot(x, r_gate[:, low:high])
-        u = dot(x, r_up[:, low:high])
-        routed_hidden[:, low:high] = silu_mul(g, u).astype(BF16)
-
-    def routed_tile(n, _):
-        columns = pl.ds(pl.multiple_of(n * 256, 256), 256)
-        o = dot(routed_hidden[...], r_down[:, columns])
-        routed_out[:, :, columns] = o.reshape(LINE, 4 * slots, 256).astype(BF16)
-        return 0
-
-    lax.fori_loop(0, width // 256, routed_tile, 0)
-
-    def second_half(zt):
+
+    def routed(first, count):
+        size = count * picked
+        base = first * picked
+        for low in range(0, hs, 256):
+            high = min(hs, low + 256)
+            g = dot(routed_x[base : base + size], r_gate[:, low:high])
+            u = dot(routed_x[base : base + size], r_up[:, low:high])
+            routed_hidden[:size, low:high] = silu_mul(g, u).astype(BF16)
+
         def tile(n, _):
             columns = pl.ds(pl.multiple_of(n * 256, 256), 256)
-            p = dot(hidden[zt], w_down[:, columns]) + dot(scatter[zt], routed_out[zt, :, columns])
+            o = dot(routed_hidden[:size], r_down[:, columns]).astype(BF16)
+            routed_out[base : base + size, columns] = o
+            return 0
+
+        lax.fori_loop(0, width // 256, tile, 0)
+
+    middle = width // 512 * 256
+    cuts = ((0, middle), (middle, width - middle))
+
+    def cut(h):
+        return pl.ds(*cuts[h])
+
+    def core_copy(zt, h):
+        return pltpu.make_async_remote_copy(
+            src_ref=part.at[zt, 1 - c, :, :, cut(h)], dst_ref=core_in.at[zt, :, :, cut(h)],
+            send_sem=rc_send.at[zt, h], recv_sem=rc_recv.at[zt, h], device_id={"expert": c_peer},
+        )
+
+    def y_copy(zt, h):
+        return pltpu.make_async_remote_copy(
+            src_ref=y_out.at[zt, :, cut(h)], dst_ref=y_in.at[zt, :, cut(h)],
+            send_sem=ry_send.at[zt, h], recv_sem=ry_recv.at[zt, h], device_id={"expert": y_peer},
+        )
+
+    def z_copy(zt, h, way, target):
+        return pltpu.make_async_remote_copy(
+            src_ref=z_out.at[zt, :, cut(h)], dst_ref=z_in.at[way, zt, :, cut(h)],
+            send_sem=rz_send.at[zt, h], recv_sem=rz_recv.at[way, zt, h], device_id={"expert": target},
+        )
+
+    def second_half(i, h):
+        zt = arrive[i]
+
+        def tile(n, _):
+            columns = pl.ds(pl.multiple_of(n * 256, 256), 256)
+            p = dot(hidden[zt], w_down[:, columns]) + dot(scatter[zt], routed_out[i * picked : (i + 1) * picked, columns])
             p = p.astype(BF16)
             for b in range(4):
                 part[zt, b % 2, b // 2, :, columns] = p[b * rows : (b + 1) * rows]
             return 0
 
-        lax.fori_loop(0, width // 256, tile, 0)
-
-    def core_copy(zt):
-        return pltpu.make_async_remote_copy(
-            src_ref=part.at[zt, 1 - c], dst_ref=core_in.at[zt], send_sem=rc_send.at[zt],
-            recv_sem=rc_recv.at[zt], device_id={"expert": c_peer},
-        )
-
-    def y_copy(zt):
-        return pltpu.make_async_remote_copy(
-            src_ref=y_out.at[zt], dst_ref=y_in.at[zt], send_sem=ry_send.at[zt],
-            recv_sem=ry_recv.at[zt], device_id={"expert": y_peer},
-        )
-
-    def z_copy(zt, way, target):
-        return pltpu.make_async_remote_copy(
-            src_ref=z_out.at[zt], dst_ref=z_in.at[way, zt], send_sem=rz_send.at[zt],
-            recv_sem=rz_recv.at[way, zt], device_id={"expert": target},
-        )
-
-    def y_stage(zt):
-        core_copy(zt).wait_recv()
-        y_out[zt] = (part[zt, c, 1 - y].astype(F32) + core_in[zt, 1 - y].astype(F32)).astype(BF16)
-        y_copy(zt).start()
-        y_keep[zt] = part[zt, c, y].astype(F32) + core_in[zt, y].astype(F32)
-
-    def z_stage(zt, last):
-        y_copy(zt).wait_recv()
-        y_keep[zt] += y_in[zt].astype(F32)
+        low, size = cuts[h]
+        lax.fori_loop(low // 256, (low + size) // 256, tile, 0)
+        core_copy(zt, h).start()
+
+    def y_stage(zt, h):
+        core_copy(zt, h).wait_recv()
+        away = part[zt, c, 1 - y, :, cut(h)].astype(F32) + core_in[zt, 1 - y, :, cut(h)].astype(F32)
+        y_out[zt, :, cut(h)] = away.astype(BF16)
+        y_copy(zt, h).start()
+        y_keep[zt, :, cut(h)] = (
+            part[zt, c, y, :, cut(h)].astype(F32) + core_in[zt, y, :, cut(h)].astype(F32)
+        )
+
+    def z_stage(zt, h, last):
+        y_copy(zt, h).wait_recv()
+        y_keep[zt, :, cut(h)] += y_in[zt, :, cut(h)].astype(F32)
 
         @pl.when((zt >= z) & (z > 0))
         def _():
-            z_copy(zt, 0, me - 4).wait_recv()
-            y_keep[zt] += z_in[0, zt].astype(F32)
+            z_copy(zt, h, 0, me - 4).wait_recv()
+            y_keep[zt, :, cut(h)] += z_in[0, zt, :, cut(h)].astype(F32)
 
         @pl.when((zt <= z) & (z < LINE - 1))
         def _():
-            z_copy(zt, 1, me + 4).wait_recv()
-            y_keep[zt] += z_in[1, zt].astype(F32)
+            z_copy(zt, h, 1, me + 4).wait_recv()
+            y_keep[zt, :, cut(h)] += z_in[1, zt, :, cut(h)].astype(F32)
 
         if last:
-            out[...] = y_keep[zt].astype(BF16)
+            out[:, cut(h)] = y_keep[zt, :, cut(h)].astype(BF16)
         else:
-            z_out[zt] = y_keep[zt].astype(BF16)
+            z_out[zt, :, cut(h)] = y_keep[zt, :, cut(h)].astype(BF16)
 
             @pl.when(zt > z)
             def _():
-                z_copy(zt, 0, me + 4).start()
+                z_copy(zt, h, 0, me + 4).start()
 
             @pl.when(zt < z)
             def _():
-                z_copy(zt, 1, me - 4).start()
+                z_copy(zt, h, 1, me - 4).start()
+
+    for h in range(2):
+        column_copies(arrive[0], h, start)
+    for load in loads:
+        load.start()
+    for h in range(2):
+        line_step(arrive[1], h)
+
+        @pl.when(near == 1)
+        def _():
+            line_step(arrive[2], h)
+
+        y_step(arrive[0], h)
+    core_step(arrive[0])
+    loads[0].wait()
+    loads[1].wait()
+    first_half(0)
+
+    for h in range(2):
+        line_step(mirror(2 + near), h)
+    for h in range(2):
+        y_step(arrive[1], h)
+    core_step(arrive[1])
+    first_half(1)
+    for load in loads[2:5]:
+        load.wait()
+    routed(0, 2)
+
+    for h in range(2):
+
+        @pl.when(near == 0)
+        def _():
+            line_step(arrive[3], h)
+
+        y_step(arrive[2], h)
+    core_step(arrive[2])
+    first_half(2)
+    routed(2, 1)
+    loads[5].wait()
+
+    for h in range(2):
+        y_step(arrive[3], h)
+        second_half(2, h)
+    for h in range(2):
+        y_stage(arrive[2], h)
+    core_step(arrive[3])
+    first_half(3)
+    routed(3, 1)
+    second_half(3, 0)
+    second_half(3, 1)
+    y_stage(arrive[3], 0)
+    second_half(1, 0)
+    y_stage(arrive[3], 1)
+    second_half(1, 1)
+    y_stage(arrive[1], 0)
+
+    @pl.when(near == 0)
+    def _():
+        for h in range(2):
+            z_stage(arrive[2], h, False)
+
+    second_half(0, 0)
+    y_stage(arrive[1], 1)
+    second_half(0, 1)
+    y_stage(arrive[0], 0)
+    y_stage(arrive[0], 1)
+
+    @pl.when(near == 1)
+    def _():
+        for h in range(2):
+            z_stage(arrive[2], h, False)
+
+    for i in range(1, LINE):
+        for h in range(2):
+            z_stage(leave[i], h, i == LINE - 1)
 
     for i in range(LINE):
-        second_half(leave[i])
-        core_copy(leave[i]).start()
-        if i > 0:
-            y_stage(leave[i - 1])
-    y_stage(leave[-1])
-    for i in range(LINE):
-        z_stage(leave[i], i == LINE - 1)
-
-    for i in range(LINE):
-        column_copies(arrive[i], wait_send)
-        block_copy(arrive[i] * 4 + (1 - y) * 2 + c, c_peer, c_send_y.at[arrive[i]]).wait_send()
-        core_copy(leave[i]).wait_send()
-        y_copy(leave[i]).wait_send()
-        if i < LINE - 1:
-            z_copy(leave[i], 0, y_peer).wait_send()
+        for h in range(2):
+            column_copies(arrive[i], h, wait_send)
+            s = arrive[i] * 4 + (1 - y) * 2 + c
+            block_copy(s, h, c_peer, c_send_y.at[arrive[i], h]).wait_send()
+            core_copy(leave[i], h).wait_send()
+            y_copy(leave[i], h).wait_send()
+            if i < LINE - 1:
+                z_copy(leave[i], h, 0, y_peer).wait_send()
 
 
 def fused(
@@ -317,11 +376,11 @@
         scratch_shapes=[
             vm((width, hid), BF16), vm((width, hid), BF16), vm((hid, width), BF16),
             vm((width, hs), BF16), vm((width, hs), BF16), vm((hs, width), BF16),
-            vm((4 * LINE, rows, width + LANES), BF16),
+            vm((4 * LINE, 2, rows // 2, width + LANES), BF16),
             vm((LINE, 4 * rows, hid), BF16),
-            vm((LINE, 4 * slots, width), BF16),
+            vm((LINE * 4 * slots, width), BF16),
             vm((LINE * 4 * slots, hs), BF16),
-            vm((LINE, 4 * slots, width), BF16),
+            vm((LINE * 4 * slots, width), BF16),
             vm((LINE, 4 * rows, 4 * slots), BF16),
             vm((LINE, 2, 2, rows, width), BF16),
             vm((LINE, 2, rows, width), BF16),
@@ -330,15 +389,16 @@
             vm((LINE, rows, width), F32),
             vm((LINE, rows, width), BF16),
             vm((2, LINE, rows, width), BF16),
-            dma((7,)), dma((4 * LINE,)), dma((LINE,)), dma((LINE,)), dma((LINE,)), dma((LINE,)),
-            dma((LINE,)),
-            dma((LINE,)), dma((LINE,)), dma((LINE,)), dma((LINE,)), dma((LINE,)), dma((2, LINE)),
+            dma((7,)), dma((4 * LINE, 2)), dma((LINE, 2)), dma((LINE, 2)), dma((LINE, 2)),
+            dma((LINE, 2)), dma((LINE, 2)),
+            dma((LINE, 2)), dma((LINE, 2)), dma((LINE, 2)), dma((LINE, 2)), dma((LINE, 2)),
+            dma((2, LINE, 2)),
         ],
         compiler_params=pltpu.CompilerParams(
             collective_id=0, has_side_effects=True, vmem_limit_bytes=60 * 1024 * 1024
         ),
         cost_estimate=pl.CostEstimate(flops=flops, bytes_accessed=21000000, transcendentals=0),
-    )(tokens, shared_gate, shared_up, shared_down, slab_gate, slab_up, slab_down, picks, counts, gates)
+    )(tokens.reshape(2, rows // 2, width), shared_gate, shared_up, shared_down, slab_gate, slab_up, slab_down, picks, counts, gates)
 
 
 def return_routed(contribution, sources, slot_count, features, onehot, experts, tok_dev):

time: 81.8 us -> 75.5 us (0.923)
  Pallas kernels: 78.6 us -> 72.3 us
    pallas_call x1, Pallas kernels: 78.6 us -> 72.3 us  [fused(): pl.pallas_call(kernel, out_shape=jax.ShapeDtypeStruct((rows, width), BF16...]
where the time goes in v2:
time: 75.5 us; the launch traced here: 75.3 us
  Pallas kernels  72.3 us (96%)
  local copies, waits for them, and re-layouts  2.96 us (4%)
    pallas_call x1, Pallas kernels, fused(): pl.pallas_call(kernel, out_shape=jax.ShapeDtypeStruct((rows, width), BF16...  72.3 us
    unnamed x2, local copies, waits for them, and re-layouts  2.96 us

profile of v2, /device:TPU:0, one launch (start us, length us, event | category | flops | bytes accessed | tf_op | source)
XLA Modules:
  0.0 75.3 jit_solution(2044992545995095107)
XLA Ops:
  0.0 1.3 %copy.11.counts = s32[8,1]{1,0:T(8,128)} copy(s32[8,1]{0,1:T(1,128)} %param.18) | data formatting | bytes 64 | tf_op args[8]
  1.3 72.3 %shard_map.100 = bf16[64,1792]{1,0:T(8,128)(2,1)} custom-call(bf16[2,32,1792]{2,1,0:T(8,128)(2,1)} %bitcast.1, bf16[1792,1280]{1,0:T(8,128)(2,1)} %shared_gate.1, bf16[1792,1280]{1,0:T(8,128)(2,1)} %shared_up.1, bf16[1280,1792]{1,0:T(8,128)(2,1)} %shared_down.1, bf16[1,1792,640]{2,1,0:T(8,128)(2,1)} %slab_gate.1, bf16[1,1792,640]{2,1,0:T(8,128)(2,1)} %slab_up.1, ...), custom_call_target="tpu_custom_call" | custom-call | flops 14092861440 | bytes 21000000 | tf_op jit(solution)/shard_map/pallas_call | solution.py:371
  73.6 1.6 %copy.13 = bf16[64,1792]{1,0:T(8,128)(2,1)} copy(bf16[64,1792]{1,0:T(8,128)(2,1)} %shard_map.100) | data formatting | bytes 458752

commit v3 on v2

--- a/solution.py
+++ b/solution.py
@@ -154,7 +154,7 @@
             hidden[zt, :, columns] = silu_mul(g, u).astype(BF16)
             return 0
 
-        lax.fori_loop(0, w_gate.shape[1] // 256, tile, 0)
+        lax.fori_loop(0, w_gate.shape[1] // 256, tile, 0, unroll=True)
         info = tok[pl.ds(zt * 4, 4), :, :, width:].reshape(4 * rows, LANES)
         slots4 = 4 * slots
         lane_r = lax.broadcasted_iota(jnp.int32, (slots4, LANES), 1)
@@ -193,7 +193,7 @@
             routed_out[base : base + size, columns] = o
             return 0
 
-        lax.fori_loop(0, width // 256, tile, 0)
+        lax.fori_loop(0, width // 256, tile, 0, unroll=True)
 
     middle = width // 512 * 256
     cuts = ((0, middle), (middle, width - middle))
@@ -231,7 +231,7 @@
             return 0
 
         low, size = cuts[h]
-        lax.fori_loop(low // 256, (low + size) // 256, tile, 0)
+        lax.fori_loop(low // 256, (low + size) // 256, tile, 0, unroll=True)
         core_copy(zt, h).start()
 
     def y_stage(zt, h):
@@ -295,7 +295,6 @@
     first_half(1)
     for load in loads[2:5]:
         load.wait()
-    routed(0, 2)
 
     for h in range(2):
 
@@ -306,12 +305,12 @@
         y_step(arrive[2], h)
     core_step(arrive[2])
     first_half(2)
-    routed(2, 1)
+    for h in range(2):
+        y_step(arrive[3], h)
+    routed(0, 3)
     loads[5].wait()
-
-    for h in range(2):
-        y_step(arrive[3], h)
-        second_half(2, h)
+    second_half(2, 0)
+    second_half(2, 1)
     for h in range(2):
         y_stage(arrive[2], h)
     core_step(arrive[3])

time: 75.5 us -> 68.3 us (0.905)
  Pallas kernels: 72.3 us -> 65.1 us
    pallas_call x1, Pallas kernels: 72.3 us -> 65.1 us  [fused(): pl.pallas_call(kernel, out_shape=jax.ShapeDtypeStruct((rows, width), BF16...]
where the time goes in v3:
time: 68.3 us; the launch traced here: 68.1 us
  Pallas kernels  65.1 us (95%)
  local copies, waits for them, and re-layouts  2.96 us (4%)
    pallas_call x1, Pallas kernels, fused(): pl.pallas_call(kernel, out_shape=jax.ShapeDtypeStruct((rows, width), BF16...  65.1 us
    unnamed x2, local copies, waits for them, and re-layouts  2.96 us

profile of v3, /device:TPU:0, one launch (start us, length us, event | category | flops | bytes accessed | tf_op | source)
XLA Modules:
  0.0 68.1 jit_solution(14331325362800569962)
XLA Ops:
  0.0 1.3 %copy.11.counts = s32[8,1]{1,0:T(8,128)} copy(s32[8,1]{0,1:T(1,128)} %param.18) | data formatting | bytes 64 | tf_op args[8]
  1.3 65.1 %shard_map.100 = bf16[64,1792]{1,0:T(8,128)(2,1)} custom-call(bf16[2,32,1792]{2,1,0:T(8,128)(2,1)} %bitcast.1, bf16[1792,1280]{1,0:T(8,128)(2,1)} %shared_gate.1, bf16[1792,1280]{1,0:T(8,128)(2,1)} %shared_up.1, bf16[1280,1792]{1,0:T(8,128)(2,1)} %shared_down.1, bf16[1,1792,640]{2,1,0:T(8,128)(2,1)} %slab_gate.1, bf16[1,1792,640]{2,1,0:T(8,128)(2,1)} %slab_up.1, ...), custom_call_target="tpu_custom_call" | custom-call | flops 14092861440 | bytes 21000000 | tf_op jit(solution)/shard_map/pallas_call | solution.py:370
  66.4 1.6 %copy.13 = bf16[64,1792]{1,0:T(8,128)(2,1)} copy(bf16[64,1792]{1,0:T(8,128)(2,1)} %shard_map.100) | data formatting | bytes 458752
